TPU v7x, 512 devices: a whole 4x8x8 slice. The times are simulated.
512 devices in a mesh: replica: 16 (over z, x_hi), fsdp: 32 (over x_lo, y, core).
Axes of the slice: x: 4 (x_hi: 2, x_lo: 2; x = x_hi * 2 + x_lo), y: 8, z: 8, core: 2. Of those that a mesh axis runs over, the one named last changes fastest.
Arguments:
- tokens: bfloat16 [131072, 8192], P(('replica', 'fsdp')), may hold values from -6 to 6
- norm_gain: float32 [8192], replicated, may hold values from 0.5 to 1.5
- weights: bfloat16 [16, 8192, 512], P('replica', 'fsdp'), may hold values from -0.0625 to 0.0625
- codes: bfloat16 [16, 8192, 512], P('replica', 'fsdp'), may hold values from -8 to 7, as said below
- scales: float32 [16, 8192, 4], P('replica', 'fsdp'), may hold values from 0.0002 to 0.003
- outer: float32 [8192, 512], P('fsdp', 'replica'), may hold values from -0.0625 to 0.0625
- momentum: float32 [8192, 512], P('fsdp', 'replica'), may hold values from -0.0625 to 0.0625
Outputs:
- keys: bfloat16 [131072, 512], P(('replica', 'fsdp'))
- outer_new: float32 [8192, 512], P('fsdp', 'replica')
- momentum_new: float32 [8192, 512], P('fsdp', 'replica')
- merged: bfloat16 [16, 8192, 512], P('replica', 'fsdp')
Inputs may be any that keep to these rules, and one draw needn't show every extreme that they name: `codes`: whole numbers.
All inputs are finite; a program needn't handle non-finite values.
Results may differ from a plain program's by a relative error of at most 0.009.
Values may be sent and summed in bfloat16 or wider, within the bound.
A program may use at most 64 MiB of HBM per device.

v0:
```python
import jax
import jax.numpy as jnp
from jax import lax
from jax.sharding import PartitionSpec as P

BLOCK = 128


def shards(tokens, norm_gain, weights, codes, scales, outer, momentum):
    values = tokens.astype(jnp.float32)
    stats = jnp.mean(values * values, axis=1, keepdims=True)
    normed = (values * lax.rsqrt(stats + 1e-05) * norm_gain).astype(jnp.bfloat16)
    own_weights = weights[0]
    local_rows = own_weights.shape[0]
    columns = own_weights.shape[1]
    total = jnp.dot(
        normed,
        lax.all_gather(own_weights, "fsdp", axis=0, tiled=True),
        preferred_element_type=jnp.float32,
    )
    keys = total.astype(jnp.bfloat16)
    block_count = columns // BLOCK
    blocks = codes[0].astype(jnp.float32).reshape(local_rows, block_count, BLOCK)
    delta = (blocks * scales[0][:, :, None]).reshape(local_rows, columns)
    summed = lax.psum_scatter(
        delta.astype(jnp.bfloat16), "replica", scatter_dimension=1, tiled=True
    ).astype(jnp.float32)
    average = summed / lax.axis_size("replica")
    moment_next = 0.9 * momentum + average
    outer_next = outer - 0.7 * (average + 0.9 * moment_next)
    gathered = lax.all_gather(outer_next, "replica", axis=1, tiled=True)
    blended = (0.5 * own_weights.astype(jnp.float32) + 0.5 * gathered).astype(jnp.bfloat16)
    outer_next, moment_next, blended = (outer_next, moment_next, blended[None])
    return (keys, outer_next, moment_next, blended)


def solution(mesh):
    in_specs = (
        P(("replica", "fsdp"), None),
        P(),
        P("replica", "fsdp", None),
        P("replica", "fsdp", None),
        P("replica", "fsdp", None),
        P("fsdp", "replica"),
        P("fsdp", "replica"),
    )
    out_specs = (
        P(("replica", "fsdp"), None),
        P("fsdp", "replica"),
        P("fsdp", "replica"),
        P("replica", "fsdp", None),
    )
    return jax.shard_map(shards, mesh=mesh, in_specs=in_specs, out_specs=out_specs, check_vma=False)
```

profile of v0, /device:TPU:16, one launch (start us, length us, event | category | flops | bytes accessed | tf_op | source)
XLA Modules:
  0.0 283.1 jit_solution(3961184429631984415)
XLA Ops:
  8.0 0.0 copy-start.1
  8.0 0.0 reduce-scatter.2.cloned.1.call-start
  8.1 1.1 copy.13
  9.1 1.4 fusion.15
  10.6 0.0 reduce-scatter.2.cloned.1.call-update
  10.6 0.0 all-gather.3.cloned.1.call-start
  10.7 0.5 all-gather.3.cloned.1.call-update
  11.2 1.1 copy.14
  12.3 3.1 %fusion = f32[256]{0:T(256)S(1)} fusion(bf16[256,8192]{1,0:T(8,128)(2,1)} %param.7), kind=kLoop, calls=%fused_computation.2 | loop fusion | flops 6291200 | bytes 4195328 | tf_op jit(solution)/shard_map/reduce_sum | solution.py:11
  15.4 209.2 %reduce-scatter.2.cloned.1.call-done = bf16[256,32]{0,1:T(8,128)(2,1)} async-done(((bf16[256,512]{0,1:T(8,128)(2,1)}), bf16[256,32]{0,1:T(8,128)(2,1)}) %reduce-scatter.2.cloned.1.call-update) | async-done | bytes 16400 | tf_op jit(solution)/shard_map/reduce_scatter | solution.py:25
  224.6 1.4 multiply_subtract_fusion
  226.0 0.0 copy-start
  226.0 41.0 %all_gather.7 = f32[256,512]{0,1:T(8,128)S(1)} all-gather(f32[256,32]{0,1:T(8,128)S(1)} %get-tuple-element.8), channel_id=1, replica_groups=mesh['replica'=16,'fsdp'=32] {'replica'}, dimensions={1}, use_global_device_ids=true | all-gather | bytes 557056 | tf_op jit(solution)/shard_map/all_gather | solution.py:31
  267.0 0.1 fusion.16
  267.1 0.8 copy.15
  267.9 0.0 all-gather.3.cloned.1.call-done
  267.9 0.0 copy-done.1
  267.9 7.8 %fusion.8 = bf16[256,512]{1,0:T(8,128)(2,1)} fusion(bf16[1,8192,512]{2,1,0:T(8,128)(2,1)} %all-gather.3.cloned.1.call-done, bf16[256,8192]{1,0:T(8,128)(2,1)} %param.7, f32[8192]{0:T(1024)S(1)} %copy-done.1, f32[256]{0:T(256)S(1)} %add_rsqrt_fusion), kind=kOutput, calls=%fused_computation.9 | convolution fusion | flops 2156003328 | bytes 12878848 | tf_op jit(solution)/shard_map/dot_general | solution.py:16
  275.7 0.0 copy-done
  (1 shorter events, 0.0 us)
Async XLA Ops:
  8.0 259.9 %copy-start.1 = (f32[8192]{0:T(1024)S(1)}, f32[8192]{0:T(1024)}, u32[]{:S(2)}) copy-start(f32[8192]{0:T(1024)} %param.8) | copy-start | bytes 98308
  8.0 216.6 %reduce-scatter.2.cloned.1.call-start = ((), (), s32[]{:S(2)}) async-start(), calls=%async_computation.1 | async-start | bytes 278528 | tf_op jit(solution)/shard_map/reduce_scatter | solution.py:25
  10.6 257.3 %all-gather.3.cloned.1.call-start = ((), (), s32[]{:S(2)}) async-start(), calls=%async_computation.2 | async-start | bytes 8650752 | tf_op jit(solution)/shard_map/all_gather | solution.py:18
  226.0 49.7 %copy-start = (f32[256,32]{0,1:T(8,128)}, f32[256,32]{0,1:T(8,128)S(1)}, u32[]{:S(2)}) copy-start(f32[256,32]{0,1:T(8,128)S(1)} %get-tuple-element.8) | copy-start | bytes 98308
Sparse Core Ops, SparseCore 0:
  13.8 210.7 reduce-scatter.1
Sparse Core Ops, SparseCore 1:
  13.2 79.6 all-gather.2
where the time goes:
time: 283 us
  waiting for transfers between devices  210 us (74%)
  blocking collectives  41 us (14%)
  between operations  15.5 us (5%)
  matrix products  7.75 us (3%)
  other arithmetic  6.03 us (2%)
  local copies, waits for them, and re-layouts  3.02 us (1%)
    reduce_scatter x1, waiting for transfers between devices, shards(): lax.psum_scatter(delta.astype(jnp.bfloat16), 'replica', scatter_dimension...  209 us
    all_gather x1, blocking collectives, shards(): gathered = lax.all_gather(outer_next, 'replica', axis=1, tiled=True)  41 us
    dot_general x1, matrix products, shards(): jnp.dot(normed, lax.all_gather(own_weights, 'fsdp', axis=0, tiled=True),...  7.75 us
  transfers between devices with their start and end apart: 2, of which 1 were waited for; matrix products, arithmetic and copies ran while one was open for 2% of the time, Pallas kernels for 0%

commit v1 on v0

v1 whole, which is shorter than its diff:
```python
import functools

import jax
import jax.numpy as jnp
from jax import lax
from jax.experimental import pallas as pl
from jax.experimental.pallas import tpu as pltpu
from jax.sharding import PartitionSpec as P

BLOCK = 128
LANES = 128
MESH = pl.DeviceIdType.MESH
F32, BF16 = jnp.float32, jnp.bfloat16


def kernel(
    ny, nz, cut,
    tok_hbm, gain_hbm, w_hbm, codes_hbm, scales_hbm, outer_hbm, mom_hbm,
    keys_hbm, outer_out_hbm, mom_out_hbm, merged_hbm,
    tok, gain, codes, scales, outer, mom, keys, merged,
    normed, full, acc, delta, parts, half, avg_blocks,
    local_in, local_out, y_send, y_recv, x_send, x_recv, d_send, d_recv,
    z_send, z_recv, g_send, g_recv, h_send, h_recv,
):
    nk = ny // 2
    rows, columns = full.shape[1], full.shape[2]
    tokens_here, width = tok.shape
    me_r, me_f = lax.axis_index("replica"), lax.axis_index("fsdp")
    z, xh = me_r // 2, me_r % 2
    xl, y, c = me_f // (2 * ny), (me_f // 2) % ny, me_f % 2

    def fsdp(col, row, core):
        return (col * ny + lax.rem(row + 2 * ny, ny)) * 2 + core

    def rep(zz, hh):
        return lax.rem(zz + 2 * nz, nz) * 2 + hh

    up, down = fsdp(xl, y + 1, c), fsdp(xl, y - 1, c)
    across, twin = fsdp(1 - xl, y, c), fsdp(xl, y, 1 - c)

    inputs = [
        pltpu.make_async_copy(w_hbm.at[0], full.at[me_f], local_in.at[0]),
        pltpu.make_async_copy(codes_hbm.at[0], codes, local_in.at[1]),
        pltpu.make_async_copy(scales_hbm, scales, local_in.at[2]),
        pltpu.make_async_copy(outer_hbm, outer, local_in.at[3]),
        pltpu.make_async_copy(mom_hbm, mom, local_in.at[4]),
        pltpu.make_async_copy(gain_hbm, gain, local_in.at[5]),
        pltpu.make_async_copy(tok_hbm, tok, local_in.at[6]),
    ]
    for copy in inputs:
        copy.start()

    barrier = pltpu.get_barrier_semaphore()
    near = [up, down, across, twin]
    far = [rep(z + j, xh) for j in range(1, nz)] + [rep(z, 1 - xh)]
    for other in near:
        pl.semaphore_signal(barrier, inc=1, device_id={"fsdp": other, "replica": me_r}, device_id_type=MESH)
    for other in far:
        pl.semaphore_signal(barrier, inc=1, device_id={"fsdp": me_f, "replica": other}, device_id_type=MESH)
    pl.semaphore_wait(barrier, len(near) + len(far))

    FIRST, SECOND, ALL = (0, cut), (cut, rows - cut), (0, rows)
    EVERY = (0, columns)
    HALF = ((0, columns // 2), (columns // 2, columns // 2))

    def region(owner, rr, cc):
        return full.at[owner, pl.ds(rr[0], rr[1]), pl.ds(cc[0], cc[1])]

    def copy_to(target, owner, rr, cc, send, recv, own=False):
        source = w_hbm.at[0, pl.ds(rr[0], rr[1]), pl.ds(cc[0], cc[1])] if own else region(owner, rr, cc)
        return pltpu.make_async_remote_copy(
            src_ref=source,
            dst_ref=region(owner, rr, cc),
            send_sem=send,
            recv_sem=recv,
            device_id={"fsdp": target, "replica": me_r},
            device_id_type=MESH,
        )

    sent = []

    def start(copy):
        copy.start()
        sent.append(copy)

    toward = (up, down)
    sign = (1, -1)

    def y_copy(d, col, k, part):
        owner = fsdp(col, y - sign[d] * (k - 1), c)
        cc = HALF[d] if k == nk else EVERY
        rr = SECOND if part == 1 else FIRST
        index = (k - 1) * 3 + part
        return copy_to(toward[d], owner, rr, cc, y_send.at[d, index], y_recv.at[d, index], own=(part < 2 and k == 1))

    def y_arrived(d, col, k, part):
        owner = fsdp(col, y - sign[d] * k, c)
        cc = HALF[d] if k == nk else EVERY
        rr = SECOND if part == 1 else FIRST
        index = (k - 1) * 3 + part
        copy_to(toward[d], owner, rr, cc, y_send.at[d, index], y_recv.at[d, index]).wait_recv()

    def x_piece(col, d, k):
        if k == 0:
            return fsdp(col, y, c), (FIRST, SECOND)[d], EVERY, d
        owner = fsdp(col, y - sign[d] * k, c)
        return owner, SECOND, HALF[d] if k == nk else EVERY, 2 * k + d

    def x_copy(d, k):
        owner, rr, cc, index = x_piece(xl, d, k)
        return copy_to(across, owner, rr, cc, x_send.at[index], x_recv.at[index], own=k == 0)

    def x_arrived(d, k):
        owner, rr, cc, index = x_piece(1 - xl, d, k)
        copy_to(across, owner, rr, cc, x_send.at[index], x_recv.at[index]).wait_recv()

    def twin_index(other, d, k):
        return other * ny + (0 if k == 0 else 2 * k - 1 + (d if k < nk else 0))

    def twin_copy(other, d, k):
        col = 1 - xl if other else xl
        index = twin_index(other, d, k)
        return copy_to(twin, fsdp(col, y - sign[d] * k, c), ALL, EVERY, d_send.at[index], d_recv.at[index],
                       own=(other == 0 and k == 0))

    def twin_arrived(other, d, k):
        col = 1 - xl if other else xl
        index = twin_index(other, d, k)
        copy_to(twin, fsdp(col, y - sign[d] * k, 1 - c), ALL, EVERY, d_send.at[index], d_recv.at[index]).wait_recv()

    def multiply(other, k, core, first=False):
        col = 1 - xl if other else xl
        count = 1 if k in (0, nk) else 2

        def one(s, carry):
            owner = fsdp(col, y - (1 - 2 * s) * k, core)
            left = normed[:, pl.ds(pl.multiple_of(owner * rows, rows), rows)]
            product = jnp.dot(left, full[owner], preferred_element_type=F32)
            if first:
                acc[...] = product
            else:
                acc[...] += product
            return carry

        lax.fori_loop(0, count, one, 0)

    for part in (0, 1):
        for d in (0, 1):
            start(y_copy(d, xl, 1, part))
        start(x_copy(part, 0))
    start(twin_copy(0, 0, 0))

    share = columns // nz
    inputs[1].wait()
    inputs[2].wait()
    for b in range(columns // BLOCK):
        block = codes[:, b * BLOCK:(b + 1) * BLOCK].astype(F32).T
        delta[b * BLOCK:(b + 1) * BLOCK, :] = (block * scales[b:b + 1, :]).astype(BF16)
    for j in range(1, nz):
        place = lax.rem(z + j, nz)
        start(pltpu.make_async_remote_copy(
            src_ref=delta.at[pl.ds(place * share, share), :],
            dst_ref=parts.at[j - 1],
            send_sem=z_send.at[j - 1], recv_sem=z_recv.at[j - 1],
            device_id={"fsdp": me_f, "replica": rep(z + j, xh)}, device_id_type=MESH,
        ))

    step_rows = 32
    chunks = width // LANES

    def norm(lo, hi):
        def one(i, carry):
            rr = pl.ds(pl.multiple_of(i * step_rows, step_rows), step_rows)
            squares = jnp.zeros((step_rows, LANES), F32)
            for j in range(chunks):
                v = tok[rr, j * LANES:(j + 1) * LANES].astype(F32)
                squares = squares + v * v
            mean = jnp.sum(squares, axis=1, keepdims=True) * (1.0 / width)
            scale = jnp.broadcast_to(lax.rsqrt(mean + 1e-05), (step_rows, LANES))
            for j in range(chunks):
                v = tok[rr, j * LANES:(j + 1) * LANES].astype(F32)
                normed[rr, j * LANES:(j + 1) * LANES] = (v * scale * gain[j:j + 1, :]).astype(BF16)
            return carry

        lax.fori_loop(lo, hi, one, 0)

    blocks = tokens_here // step_rows
    inputs[5].wait()
    inputs[6].wait()
    inputs[0].wait()
    norm(0, blocks // 2)

    def pass_on(k, part):
        for d in (0, 1):
            y_arrived(d, xl, k, part)
            if k < nk:
                start(y_copy(d, xl, k + 1, part))
        if part == 1:
            for d in (0, 1):
                start(x_copy(d, k))
            for d in (0, 1) if k < nk else (0,):
                start(twin_copy(0, d, k))

    def pass_other(k):
        for d in (0, 1):
            y_arrived(d, 1 - xl, k, 2)
            if k < nk:
                start(y_copy(d, 1 - xl, k + 1, 2))
        for d in (0, 1):
            x_arrived(d, k)
        for d in (0, 1) if k < nk else (0,):
            start(twin_copy(1, d, k))

    def take(other, k):
        for d in (0, 1) if 0 < k < nk else (0,):
            twin_arrived(other, d, k)
        multiply(other, k, 1 - c)

    n_rep = nz * 2
    slim = columns // n_rep

    def outer_sum():
        for j in range(1, nz):
            pltpu.make_async_remote_copy(
                src_ref=parts.at[j - 1], dst_ref=parts.at[j - 1],
                send_sem=z_send.at[j - 1], recv_sem=z_recv.at[j - 1],
                device_id={"fsdp": me_f, "replica": rep(z + j, xh)}, device_id_type=MESH,
            ).wait_recv()

        def total(which):
            lo = pl.multiple_of(z * share + which * slim, slim)
            value = delta[pl.ds(lo, slim), :].astype(F32)
            for j in range(1, nz):
                value = value + parts[j - 1, pl.ds(pl.multiple_of(which * slim, slim), slim), :].astype(F32)
            return value

        half[0] = total(1 - xh).astype(BF16)
        start(half_copy())
        return total(xh)

    def half_copy():
        return pltpu.make_async_remote_copy(
            src_ref=half.at[0], dst_ref=half.at[1], send_sem=h_send.at[0], recv_sem=h_recv.at[0],
            device_id={"fsdp": me_f, "replica": rep(z, 1 - xh)}, device_id_type=MESH,
        )

    def slim_copy(owner):
        ref = avg_blocks.at[pl.ds(pl.multiple_of(owner * slim, slim), slim), :]
        return pltpu.make_async_remote_copy(
            src_ref=ref, dst_ref=ref, send_sem=h_send.at[1], recv_sem=h_recv.at[1],
            device_id={"fsdp": me_f, "replica": rep(z, 1 - xh)}, device_id_type=MESH,
        )

    def share_copy(owner_z, j):
        ref = avg_blocks.at[pl.ds(pl.multiple_of(owner_z * share, share), share), :]
        return pltpu.make_async_remote_copy(
            src_ref=ref, dst_ref=ref, send_sem=g_send.at[j - 1], recv_sem=g_recv.at[j - 1],
            device_id={"fsdp": me_f, "replica": rep(z + j, xh)}, device_id_type=MESH,
        )

    outputs = [
        pltpu.make_async_copy(outer, outer_out_hbm, local_out.at[0]),
        pltpu.make_async_copy(mom, mom_out_hbm, local_out.at[1]),
        pltpu.make_async_copy(merged, merged_hbm.at[0], local_out.at[2]),
        pltpu.make_async_copy(keys, keys_hbm, local_out.at[3]),
    ]

    def outer_step(mine):
        half_copy().wait_recv()
        inputs[3].wait()
        inputs[4].wait()
        average = (mine + half[1].astype(F32)) * (1.0 / n_rep)
        moment = 0.9 * mom[...] + average
        stepped = outer[...] - 0.7 * (average + 0.9 * moment)
        mom[...] = moment
        outer[...] = stepped
        avg_blocks[pl.ds(pl.multiple_of(me_r * slim, slim), slim), :] = stepped.astype(BF16)
        start(slim_copy(me_r))
        outputs[0].start()
        outputs[1].start()

    def outer_spread():
        slim_copy(rep(z, 1 - xh)).wait_recv()
        for j in range(1, nz):
            start(share_copy(z, j))

    def outer_merge():
        for j in range(1, nz):
            share_copy(lax.rem(z - j + nz, nz), j).wait_recv()
        for b in range(columns // LANES):
            block = avg_blocks[b * LANES:(b + 1) * LANES, :].astype(F32).T
            own = full[me_f, :, b * LANES:(b + 1) * LANES].astype(F32)
            merged[:, b * LANES:(b + 1) * LANES] = (0.5 * own + 0.5 * block).astype(BF16)
        outputs[2].start()

    pass_on(1, 0)
    norm(blocks // 2, blocks)
    pass_on(1, 1)
    for part in (0, 1):
        x_arrived(part, 0)
    start(twin_copy(1, 0, 0))
    multiply(0, 0, c, first=True)
    mine = outer_sum()
    multiply(0, 1, c)
    take(0, 0)
    pass_on(2, 0)
    outer_step(mine)
    multiply(1, 0, c)
    take(0, 1)
    outer_spread()
    pass_on(2, 1)
    take(1, 0)
    for k in range(3, nk + 1):
        pass_on(k, 0)
        multiply(0, k - 1, c)
        take(0, k - 1)
        if k == nk:
            for d in (0, 1):
                start(y_copy(d, 1 - xl, 1, 2))
            outer_merge()
        pass_on(k, 1)
    multiply(0, nk, c)
    for k in range(1, nk + 1):
        pass_other(k)
        take(k > 1, max(k - 1, 0) if k > 1 else nk)
        multiply(1, k, c)
    take(1, nk)
    keys[...] = acc[...].astype(BF16)
    outputs[3].start()
    for copy in sent:
        copy.wait_send()
    for copy in outputs:
        copy.wait()


def shards(ny, nz, tokens, norm_gain, weights, codes, scales, outer, momentum):
    tokens_here, width = tokens.shape
    _, rows, columns = weights.shape
    n_fsdp, n_rep = 4 * ny, 2 * nz
    slim, share = columns // n_rep, columns // nz
    nk = ny // 2
    cut = rows * 7 // 16
    anywhere = pl.BlockSpec(memory_space=pl.ANY)
    dma = pltpu.SemaphoreType.DMA
    keys, outer_next, moment_next, merged = pl.pallas_call(
        functools.partial(kernel, ny, nz, cut),
        out_shape=(
            jax.ShapeDtypeStruct((tokens_here, columns), BF16),
            jax.ShapeDtypeStruct((slim, rows), F32),
            jax.ShapeDtypeStruct((slim, rows), F32),
            jax.ShapeDtypeStruct((1, rows, columns), BF16),
        ),
        in_specs=[anywhere] * 7,
        out_specs=(anywhere,) * 4,
        scratch_shapes=[
            pltpu.VMEM((tokens_here, width), BF16),
            pltpu.VMEM((width // LANES, LANES), F32),
            pltpu.VMEM((rows, columns), BF16),
            pltpu.VMEM((columns // BLOCK, rows), F32),
            pltpu.VMEM((slim, rows), F32),
            pltpu.VMEM((slim, rows), F32),
            pltpu.VMEM((tokens_here, columns), BF16),
            pltpu.VMEM((rows, columns), BF16),
            pltpu.VMEM((tokens_here, width), BF16),
            pltpu.VMEM((n_fsdp, rows, columns), BF16),
            pltpu.VMEM((tokens_here, columns), F32),
            pltpu.VMEM((columns, rows), BF16),
            pltpu.VMEM((nz - 1, share, rows), BF16),
            pltpu.VMEM((2, slim, rows), BF16),
            pltpu.VMEM((columns, rows), BF16),
            dma((7,)), dma((4,)),
            dma((2, 3 * nk)), dma((2, 3 * nk)),
            dma((2 * nk + 2,)), dma((2 * nk + 2,)),
            dma((2 * ny,)), dma((2 * ny,)),
            dma((nz - 1,)), dma((nz - 1,)),
            dma((nz - 1,)), dma((nz - 1,)),
            dma((2,)), dma((2,)),
        ],
        compiler_params=pltpu.CompilerParams(
            collective_id=0, has_side_effects=True, vmem_limit_bytes=60 * 1024 * 1024
        ),
        cost_estimate=pl.CostEstimate(
            flops=2 * tokens_here * width * columns, bytes_accessed=2 * tokens_here * width, transcendentals=0
        ),
    )(
        tokens,
        norm_gain.reshape(width // LANES, LANES),
        weights,
        codes,
        scales[0].T,
        outer.T,
        momentum.T,
    )
    return keys, outer_next.T, moment_next.T, merged


def solution(mesh):
    in_specs = (
        P(("replica", "fsdp"), None),
        P(),
        P("replica", "fsdp", None),
        P("replica", "fsdp", None),
        P("replica", "fsdp", None),
        P("fsdp", "replica"),
        P("fsdp", "replica"),
    )
    out_specs = (
        P(("replica", "fsdp"), None),
        P("fsdp", "replica"),
        P("fsdp", "replica"),
        P("replica", "fsdp", None),
    )
    ny, nz = mesh.shape["fsdp"] // 4, mesh.shape["replica"] // 2
    return jax.shard_map(
        functools.partial(shards, ny, nz), mesh=mesh, in_specs=in_specs, out_specs=out_specs, check_vma=False
    )
```

time: 283 us -> 67.3 us (0.24)
  the two profiles are of different devices: /device:TPU:16 before, /device:TPU:1 now
where the time goes in v1:
time: 67.3 us; the launch traced here: 67 us
  Pallas kernels  60.3 us (90%)
  local copies, waits for them, and re-layouts  6.09 us (9%)
    pallas_call x1, Pallas kernels, shards(): pl.pallas_call(functools.partial(kernel, ny, nz, cut), out_shape=(jax.Sha...  60.3 us
    unnamed x4, local copies, waits for them, and re-layouts  6.09 us

profile of v1, /device:TPU:1, one launch (start us, length us, event | category | flops | bytes accessed | tf_op | source)
XLA Modules:
  0.0 67.0 jit_solution(13306839624354910770)
XLA Ops:
  0.6 60.3 %shard_map.102 = (bf16[256,512]{1,0:T(8,128)(2,1)}, f32[32,256]{1,0:T(8,128)}, f32[32,256]{1,0:T(8,128)}, bf16[1,256,512]{2,1,0:T(8,128)(2,1)}) custom-call(bf16[256,8192]{1,0:T(8,128)(2,1)} %tok_hbm.1, f32[64,128]{1,0:T(8,128)} %bitcast.10, bf16[1,256,512]{2,1,0:T(8,128)(2,1)} %w_hbm.1, bf16[1,256,512]{2,1,0:T(8,128)(2,1)} %codes_hbm.1, f32[4,256]{1,0:T(4,128)} %bitcast.13, ...), custom_call_target="tpu_custom_call" | custom-call | flops 2147483648 | bytes 4194304 | tf_op jit(solution)/shard_map/pallas_call | solution.py:345
  60.9 1.7 %copy.15 = bf16[256,512]{1,0:T(8,128)(2,1)} copy(bf16[256,512]{1,0:T(8,128)(2,1)} %get-tuple-element.16) | data formatting | bytes 524288
  62.6 1.4 %copy.16 = f32[256,32]{0,1:T(8,128)} copy(f32[256,32]{0,1:T(8,128)} %bitcast.9) | data formatting | bytes 65536
  64.0 1.4 %copy.17 = f32[256,32]{0,1:T(8,128)} copy(f32[256,32]{0,1:T(8,128)} %bitcast.8) | data formatting | bytes 65536
  65.3 1.7 %copy.18 = bf16[1,256,512]{2,1,0:T(8,128)(2,1)} copy(bf16[1,256,512]{2,1,0:T(8,128)(2,1)} %get-tuple-element.19) | data formatting | bytes 524288

commit v2 on v1

--- a/solution.py
+++ b/solution.py
@@ -16,11 +16,11 @@
 def kernel(
     ny, nz, cut,
     tok_hbm, gain_hbm, w_hbm, codes_hbm, scales_hbm, outer_hbm, mom_hbm,
-    keys_hbm, outer_out_hbm, mom_out_hbm, merged_hbm,
-    tok, gain, codes, scales, outer, mom, keys, merged,
+    keys, outer_out, mom_out, merged,
+    tok, gain, codes, scales, outer, mom,
     normed, full, acc, delta, parts, half, avg_blocks,
-    local_in, local_out, y_send, y_recv, x_send, x_recv, d_send, d_recv,
-    z_send, z_recv, g_send, g_recv, h_send, h_recv,
+    local_in, y_send, y_recv, x_send, x_recv, d_send, d_recv,
+    z_send, z_recv, g_send, g_recv, h_send, h_recv, near_sem, far_sem,
 ):
     nk = ny // 2
     rows, columns = full.shape[1], full.shape[2]
@@ -53,11 +53,35 @@
     barrier = pltpu.get_barrier_semaphore()
     near = [up, down, across, twin]
     far = [rep(z + j, xh) for j in range(1, nz)] + [rep(z, 1 - xh)]
-    for other in near:
-        pl.semaphore_signal(barrier, inc=1, device_id={"fsdp": other, "replica": me_r}, device_id_type=MESH)
-    for other in far:
-        pl.semaphore_signal(barrier, inc=1, device_id={"fsdp": me_f, "replica": other}, device_id_type=MESH)
-    pl.semaphore_wait(barrier, len(near) + len(far))
+    odd = lax.rem(xl + y + c, 2) == 1
+    late = z >= nz // 2
+
+    @pl.when(odd)
+    def _():
+        for other in near:
+            pl.semaphore_signal(barrier, inc=1, device_id={"fsdp": other, "replica": me_r}, device_id_type=MESH)
+
+    @pl.when(jnp.logical_not(odd))
+    def _():
+        pl.semaphore_wait(barrier, len(near))
+        for other in near:
+            pl.semaphore_signal(near_sem, inc=1, device_id={"fsdp": other, "replica": me_r}, device_id_type=MESH)
+
+    @pl.when(odd)
+    def _():
+        pl.semaphore_wait(near_sem, len(near))
+        for other in far:
+            pl.semaphore_signal(barrier, inc=1, device_id={"fsdp": me_f, "replica": other}, device_id_type=MESH)
+
+    def meet_far():
+        @pl.when(odd)
+        def _():
+            pl.semaphore_wait(barrier, len(far))
+            pl.semaphore_signal(far_sem, inc=1, device_id={"fsdp": twin, "replica": me_r}, device_id_type=MESH)
+
+        @pl.when(jnp.logical_not(odd))
+        def _():
+            pl.semaphore_wait(far_sem, 1)
 
     FIRST, SECOND, ALL = (0, cut), (cut, rows - cut), (0, rows)
     EVERY = (0, columns)
@@ -156,14 +180,23 @@
     for b in range(columns // BLOCK):
         block = codes[:, b * BLOCK:(b + 1) * BLOCK].astype(F32).T
         delta[b * BLOCK:(b + 1) * BLOCK, :] = (block * scales[b:b + 1, :]).astype(BF16)
-    for j in range(1, nz):
-        place = lax.rem(z + j, nz)
-        start(pltpu.make_async_remote_copy(
-            src_ref=delta.at[pl.ds(place * share, share), :],
+    reduce_copies = [
+        pltpu.make_async_remote_copy(
+            src_ref=delta.at[pl.ds(pl.multiple_of(lax.rem(z + j, nz) * share, share), share), :],
             dst_ref=parts.at[j - 1],
             send_sem=z_send.at[j - 1], recv_sem=z_recv.at[j - 1],
             device_id={"fsdp": me_f, "replica": rep(z + j, xh)}, device_id_type=MESH,
-        ))
+        )
+        for j in range(1, nz)
+    ]
+    sent.extend(reduce_copies)
+
+    def outer_send():
+        meet_far()
+        for copy in reduce_copies:
+            copy.start()
+
+    pl.when(late)(outer_send)
 
     step_rows = 32
     chunks = width // LANES
@@ -190,29 +223,37 @@
     inputs[0].wait()
     norm(0, blocks // 2)
 
-    def pass_on(k, part):
+    def ways(k):
+        return (0, 1) if k < nk else (0,)
+
+    def pass_own(k):
+        for part in (0, 1):
+            for d in (0, 1):
+                y_arrived(d, xl, k, part)
+                if k < nk:
+                    start(y_copy(d, xl, k + 1, part))
         for d in (0, 1):
-            y_arrived(d, xl, k, part)
-            if k < nk:
-                start(y_copy(d, xl, k + 1, part))
-        if part == 1:
-            for d in (0, 1):
-                start(x_copy(d, k))
-            for d in (0, 1) if k < nk else (0,):
-                start(twin_copy(0, d, k))
-
-    def pass_other(k):
+            start(x_copy(d, k))
+        for d in ways(k):
+            start(twin_copy(0, d, k))
+
+    def pass_first(k):
         for d in (0, 1):
-            y_arrived(d, 1 - xl, k, 2)
-            if k < nk:
-                start(y_copy(d, 1 - xl, k + 1, 2))
+            if k == 0:
+                start(y_copy(d, 1 - xl, 1, 2))
+            else:
+                y_arrived(d, 1 - xl, k, 2)
+                if k < nk:
+                    start(y_copy(d, 1 - xl, k + 1, 2))
+
+    def complete(k):
         for d in (0, 1):
             x_arrived(d, k)
-        for d in (0, 1) if k < nk else (0,):
+        for d in ways(k):
             start(twin_copy(1, d, k))
 
     def take(other, k):
-        for d in (0, 1) if 0 < k < nk else (0,):
+        for d in ways(k) if k else (0,):
             twin_arrived(other, d, k)
         multiply(other, k, 1 - c)
 
@@ -258,13 +299,6 @@
             device_id={"fsdp": me_f, "replica": rep(z + j, xh)}, device_id_type=MESH,
         )
 
-    outputs = [
-        pltpu.make_async_copy(outer, outer_out_hbm, local_out.at[0]),
-        pltpu.make_async_copy(mom, mom_out_hbm, local_out.at[1]),
-        pltpu.make_async_copy(merged, merged_hbm.at[0], local_out.at[2]),
-        pltpu.make_async_copy(keys, keys_hbm, local_out.at[3]),
-    ]
-
     def outer_step(mine):
         half_copy().wait_recv()
         inputs[3].wait()
@@ -272,17 +306,17 @@
         average = (mine + half[1].astype(F32)) * (1.0 / n_rep)
         moment = 0.9 * mom[...] + average
         stepped = outer[...] - 0.7 * (average + 0.9 * moment)
-        mom[...] = moment
-        outer[...] = stepped
+        mom_out[...] = moment
+        outer_out[...] = stepped
         avg_blocks[pl.ds(pl.multiple_of(me_r * slim, slim), slim), :] = stepped.astype(BF16)
         start(slim_copy(me_r))
-        outputs[0].start()
-        outputs[1].start()
+
+    spread_copies = [share_copy(z, j) for j in range(1, nz)]
 
     def outer_spread():
         slim_copy(rep(z, 1 - xh)).wait_recv()
-        for j in range(1, nz):
-            start(share_copy(z, j))
+        for copy in spread_copies:
+            copy.start()
 
     def outer_merge():
         for j in range(1, nz):
@@ -290,46 +324,63 @@
         for b in range(columns // LANES):
             block = avg_blocks[b * LANES:(b + 1) * LANES, :].astype(F32).T
             own = full[me_f, :, b * LANES:(b + 1) * LANES].astype(F32)
-            merged[:, b * LANES:(b + 1) * LANES] = (0.5 * own + 0.5 * block).astype(BF16)
-        outputs[2].start()
-
-    pass_on(1, 0)
+            merged[0, :, b * LANES:(b + 1) * LANES] = (0.5 * own + 0.5 * block).astype(BF16)
+
+    pass_own(1)
+    pl.when(jnp.logical_not(late))(outer_send)
     norm(blocks // 2, blocks)
-    pass_on(1, 1)
-    for part in (0, 1):
-        x_arrived(part, 0)
+    x_arrived(0, 0)
+    x_arrived(1, 0)
     start(twin_copy(1, 0, 0))
     multiply(0, 0, c, first=True)
+    take(0, 0)
+    pass_own(2)
+    pass_first(0)
     mine = outer_sum()
     multiply(0, 1, c)
-    take(0, 0)
-    pass_on(2, 0)
-    outer_step(mine)
     multiply(1, 0, c)
     take(0, 1)
-    outer_spread()
-    pass_on(2, 1)
+    outer_step(mine)
     take(1, 0)
-    for k in range(3, nk + 1):
-        pass_on(k, 0)
-        multiply(0, k - 1, c)
-        take(0, k - 1)
-        if k == nk:
-            for d in (0, 1):
-                start(y_copy(d, 1 - xl, 1, 2))
-            outer_merge()
-        pass_on(k, 1)
-    multiply(0, nk, c)
-    for k in range(1, nk + 1):
-        pass_other(k)
-        take(k > 1, max(k - 1, 0) if k > 1 else nk)
-        multiply(1, k, c)
-    take(1, nk)
+    pl.when(late)(outer_spread)
+    pass_own(3)
+    sent.extend(spread_copies)
+    pl.when(jnp.logical_not(late))(outer_spread)
+    multiply(0, 2, c)
+    take(0, 2)
+    pass_first(1)
+    multiply(0, 3, c)
+    pass_own(4)
+    take(0, 3)
+    pass_first(2)
+    complete(1)
+    multiply(0, 4, c)
+    multiply(1, 1, c)
+    take(0, 4)
+    pass_first(3)
+    complete(2)
+    multiply(1, 2, c)
+    take(1, 1)
+    complete(3)
+    multiply(1, 3, c)
+    take(1, 2)
+    outer_merge()
+    take(1, 3)
+    pass_first(4)
+    complete(4)
+    multiply(1, 4, c)
+    take(1, 4)
     keys[...] = acc[...].astype(BF16)
-    outputs[3].start()
     for copy in sent:
         copy.wait_send()
-    for copy in outputs:
+
+
+def write(keys, outer, mom, merged, keys_out, outer_out, mom_out, merged_out, sems):
+    pairs = ((keys, keys_out), (outer, outer_out), (mom, mom_out), (merged, merged_out))
+    copies = [pltpu.make_async_copy(a, b, sems.at[i]) for i, (a, b) in enumerate(pairs)]
+    for copy in copies:
+        copy.start()
+    for copy in copies:
         copy.wait()
 
 
@@ -339,19 +390,21 @@
     n_fsdp, n_rep = 4 * ny, 2 * nz
     slim, share = columns // n_rep, columns // nz
     nk = ny // 2
-    cut = rows * 7 // 16
-    anywhere = pl.BlockSpec(memory_space=pl.ANY)
+    cut = rows // 2
+    hbm = pl.BlockSpec(memory_space=pltpu.HBM)
+    vmem = pl.BlockSpec(memory_space=pltpu.VMEM)
     dma = pltpu.SemaphoreType.DMA
-    keys, outer_next, moment_next, merged = pl.pallas_call(
+    results = (
+        ((tokens_here, columns), BF16),
+        ((slim, rows), F32),
+        ((slim, rows), F32),
+        ((1, rows, columns), BF16),
+    )
+    held = pl.pallas_call(
         functools.partial(kernel, ny, nz, cut),
-        out_shape=(
-            jax.ShapeDtypeStruct((tokens_here, columns), BF16),
-            jax.ShapeDtypeStruct((slim, rows), F32),
-            jax.ShapeDtypeStruct((slim, rows), F32),
-            jax.ShapeDtypeStruct((1, rows, columns), BF16),
-        ),
-        in_specs=[anywhere] * 7,
-        out_specs=(anywhere,) * 4,
+        out_shape=tuple(pltpu.VMEM(shape, dtype) for shape, dtype in results),
+        in_specs=[hbm] * 7,
+        out_specs=(vmem,) * 4,
         scratch_shapes=[
             pltpu.VMEM((tokens_here, width), BF16),
             pltpu.VMEM((width // LANES, LANES), F32),
@@ -359,8 +412,6 @@
             pltpu.VMEM((columns // BLOCK, rows), F32),
             pltpu.VMEM((slim, rows), F32),
             pltpu.VMEM((slim, rows), F32),
-            pltpu.VMEM((tokens_here, columns), BF16),
-            pltpu.VMEM((rows, columns), BF16),
             pltpu.VMEM((tokens_here, width), BF16),
             pltpu.VMEM((n_fsdp, rows, columns), BF16),
             pltpu.VMEM((tokens_here, columns), F32),
@@ -368,13 +419,14 @@
             pltpu.VMEM((nz - 1, share, rows), BF16),
             pltpu.VMEM((2, slim, rows), BF16),
             pltpu.VMEM((columns, rows), BF16),
-            dma((7,)), dma((4,)),
+            dma((7,)),
             dma((2, 3 * nk)), dma((2, 3 * nk)),
             dma((2 * nk + 2,)), dma((2 * nk + 2,)),
             dma((2 * ny,)), dma((2 * ny,)),
             dma((nz - 1,)), dma((nz - 1,)),
             dma((nz - 1,)), dma((nz - 1,)),
             dma((2,)), dma((2,)),
+            pltpu.SemaphoreType.REGULAR, pltpu.SemaphoreType.REGULAR,
         ],
         compiler_params=pltpu.CompilerParams(
             collective_id=0, has_side_effects=True, vmem_limit_bytes=60 * 1024 * 1024
@@ -391,6 +443,14 @@
         outer.T,
         momentum.T,
     )
+    keys, outer_next, moment_next, merged = pl.pallas_call(
+        write,
+        out_shape=tuple(jax.ShapeDtypeStruct(shape, dtype) for shape, dtype in results),
+        in_specs=[vmem] * 4,
+        out_specs=(hbm,) * 4,
+        scratch_shapes=[dma((4,))],
+        compiler_params=pltpu.CompilerParams(vmem_limit_bytes=4 * 1024 * 1024),
+    )(*held)
     return keys, outer_next.T, moment_next.T, merged
 
 

time: 67.3 us -> 52 us (0.77)
  Pallas kernels: 60.3 us -> 51.2 us
  local copies, waits for them, and re-layouts: 6.09 us -> 0 us
    pallas_call x1 -> x2, Pallas kernels: 60.3 us -> 51.2 us  [the longest x1 50.4 us: shards(): pl.pallas_call(functools.partial(kernel, ny, nz, cut), out_shape=tuple((p...]
    unnamed x4 -> x0, local copies, waits for them, and re-layouts: 6.09 us -> none
where the time goes in v2:
time: 52 us; the launch traced here: 51.9 us
  Pallas kernels  51.2 us (98%)
  between operations  0.64 us (1%)
    pallas_call x1, Pallas kernels, shards(): pl.pallas_call(functools.partial(kernel, ny, nz, cut), out_shape=tuple((p...  50.4 us

profile of v2, /device:TPU:1, one launch (start us, length us, event | category | flops | bytes accessed | tf_op | source)
XLA Modules:
  0.0 51.9 jit_solution(10516258203551246384)
XLA Ops:
  0.6 50.4 %shard_map.102 = (bf16[256,512]{1,0:T(8,128)(2,1)S(1)}, f32[32,256]{1,0:T(8,128)S(1)}, f32[32,256]{1,0:T(8,128)S(1)}, bf16[1,256,512]{2,1,0:T(8,128)(2,1)S(1)}) custom-call(bf16[256,8192]{1,0:T(8,128)(2,1)} %tok_hbm.1, f32[64,128]{1,0:T(8,128)} %bitcast.8, bf16[1,256,512]{2,1,0:T(8,128)(2,1)} %w_hbm.1, bf16[1,256,512]{2,1,0:T(8,128)(2,1)} %codes_hbm.1, ...), custom_call_target="tpu_custom_call" | custom-call | flops 2147483648 | bytes 4194304 | tf_op jit(solution)/shard_map/pallas_call | solution.py:403
  51.0 0.8 %shard_map.103 = (bf16[256,512]{1,0:T(8,128)(2,1)}, f32[32,256]{1,0:T(8,128)}, f32[32,256]{1,0:T(8,128)}, bf16[1,256,512]{2,1,0:T(8,128)(2,1)}) custom-call(bf16[256,512]{1,0:T(8,128)(2,1)S(1)} %get-tuple-element.12.keys, f32[32,256]{1,0:T(8,128)S(1)} %get-tuple-element.13.outer, f32[32,256]{1,0:T(8,128)S(1)} %get-tuple-element.14.mom, ...), custom_call_target="tpu_custom_call" | custom-call | tf_op jit(solution)/shard_map/pallas_call | solution.py:446

commit v3 on v2

--- a/solution.py
+++ b/solution.py
@@ -10,6 +10,13 @@
 BLOCK = 128
 LANES = 128
 MESH = pl.DeviceIdType.MESH
+ORDER = (
+    "l0", "n0", "G1", "F1", "T1", "e0", "P0", "n1", "X0", "M0", "t0", "l1",
+    "G2", "F2", "T2", "P1", "e1", "l2", "M1", "N0", "t1", "e2", "x0", "l3",
+    "G3", "P2", "F3", "T3", "e3", "M2", "t2", "M3", "G4", "X1", "F4", "T4",
+    "t3", "P3", "M4", "N1", "t4", "X2", "N2", "x1", "X3", "N3", "x2", "P4",
+    "X4", "Z0", "N4", "x3", "x4",
+)
 F32, BF16 = jnp.float32, jnp.bfloat16
 
 
@@ -18,7 +25,7 @@
     tok_hbm, gain_hbm, w_hbm, codes_hbm, scales_hbm, outer_hbm, mom_hbm,
     keys, outer_out, mom_out, merged,
     tok, gain, codes, scales, outer, mom,
-    normed, full, acc, delta, parts, half, avg_blocks,
+    normed, full, acc, delta, parts, half, avg_blocks, mine,
     local_in, y_send, y_recv, x_send, x_recv, d_send, d_recv,
     z_send, z_recv, g_send, g_recv, h_send, h_recv, near_sem, far_sem,
 ):
@@ -168,10 +175,12 @@
 
         lax.fori_loop(0, count, one, 0)
 
-    for part in (0, 1):
-        for d in (0, 1):
-            start(y_copy(d, xl, 1, part))
-        start(x_copy(part, 0))
+    start(x_copy(0, 0))
+    for d in (0, 1):
+        start(y_copy(d, xl, 1, 1))
+    for d in (0, 1):
+        start(y_copy(d, xl, 1, 0))
+    start(x_copy(1, 0))
     start(twin_copy(0, 0, 0))
 
     share = columns // nz
@@ -196,7 +205,6 @@
         for copy in reduce_copies:
             copy.start()
 
-    pl.when(late)(outer_send)
 
     step_rows = 32
     chunks = width // LANES
@@ -218,28 +226,32 @@
         lax.fori_loop(lo, hi, one, 0)
 
     blocks = tokens_here // step_rows
+    inputs[3].wait()
+    inputs[4].wait()
     inputs[5].wait()
     inputs[6].wait()
     inputs[0].wait()
-    norm(0, blocks // 2)
-
     def ways(k):
         return (0, 1) if k < nk else (0,)
 
-    def pass_own(k):
-        for part in (0, 1):
+    def pass_own(k, part):
+        for d in (0, 1):
+            y_arrived(d, xl, k, part)
+            if k < nk:
+                start(y_copy(d, xl, k + 1, part))
+        if part == 1:
             for d in (0, 1):
-                y_arrived(d, xl, k, part)
-                if k < nk:
-                    start(y_copy(d, xl, k + 1, part))
-        for d in (0, 1):
-            start(x_copy(d, k))
+                start(x_copy(d, k))
+
+    def own_to_twin(k):
         for d in ways(k):
             start(twin_copy(0, d, k))
 
     def pass_first(k):
         for d in (0, 1):
             if k == 0:
+                if d == 0:
+                    x_arrived(0, 0)
                 start(y_copy(d, 1 - xl, 1, 2))
             else:
                 y_arrived(d, 1 - xl, k, 2)
@@ -247,9 +259,9 @@
                     start(y_copy(d, 1 - xl, k + 1, 2))
 
     def complete(k):
-        for d in (0, 1):
+        for d in (0, 1) if k else (1,):
             x_arrived(d, k)
-        for d in ways(k):
+        for d in ways(k) if k else (0,):
             start(twin_copy(1, d, k))
 
     def take(other, k):
@@ -276,8 +288,8 @@
             return value
 
         half[0] = total(1 - xh).astype(BF16)
-        start(half_copy())
-        return total(xh)
+        half_copy().start()
+        mine[...] = total(xh)
 
     def half_copy():
         return pltpu.make_async_remote_copy(
@@ -299,17 +311,18 @@
             device_id={"fsdp": me_f, "replica": rep(z + j, xh)}, device_id_type=MESH,
         )
 
-    def outer_step(mine):
+    slim_out = slim_copy(me_r)
+    sent.extend([half_copy(), slim_out])
+
+    def outer_step():
         half_copy().wait_recv()
-        inputs[3].wait()
-        inputs[4].wait()
-        average = (mine + half[1].astype(F32)) * (1.0 / n_rep)
+        average = (mine[...] + half[1].astype(F32)) * (1.0 / n_rep)
         moment = 0.9 * mom[...] + average
         stepped = outer[...] - 0.7 * (average + 0.9 * moment)
         mom_out[...] = moment
         outer_out[...] = stepped
         avg_blocks[pl.ds(pl.multiple_of(me_r * slim, slim), slim), :] = stepped.astype(BF16)
-        start(slim_copy(me_r))
+        slim_out.start()
 
     spread_copies = [share_copy(z, j) for j in range(1, nz)]
 
@@ -326,50 +339,25 @@
             own = full[me_f, :, b * LANES:(b + 1) * LANES].astype(F32)
             merged[0, :, b * LANES:(b + 1) * LANES] = (0.5 * own + 0.5 * block).astype(BF16)
 
-    pass_own(1)
-    pl.when(jnp.logical_not(late))(outer_send)
-    norm(blocks // 2, blocks)
-    x_arrived(0, 0)
-    x_arrived(1, 0)
-    start(twin_copy(1, 0, 0))
-    multiply(0, 0, c, first=True)
-    take(0, 0)
-    pass_own(2)
-    pass_first(0)
-    mine = outer_sum()
-    multiply(0, 1, c)
-    multiply(1, 0, c)
-    take(0, 1)
-    outer_step(mine)
-    take(1, 0)
-    pl.when(late)(outer_spread)
-    pass_own(3)
+    early = jnp.logical_not(late)
+    steps = {
+        "F": lambda k: pass_own(k, 0),
+        "G": lambda k: pass_own(k, 1),
+        "T": own_to_twin,
+        "P": pass_first,
+        "X": complete,
+        "M": lambda k: multiply(0, k, c, first=k == 0),
+        "N": lambda k: multiply(1, k, c),
+        "t": lambda k: take(0, k),
+        "x": lambda k: take(1, k),
+        "n": lambda k: norm(blocks * k // 2, blocks * (k + 1) // 2),
+        "e": lambda k: pl.when(early)((outer_send, outer_sum, outer_step, outer_spread)[k]),
+        "l": lambda k: pl.when(late)((outer_send, outer_sum, outer_step, outer_spread)[k]),
+        "Z": lambda k: outer_merge(),
+    }
+    for step in ORDER:
+        steps[step[0]](int(step[1]))
     sent.extend(spread_copies)
-    pl.when(jnp.logical_not(late))(outer_spread)
-    multiply(0, 2, c)
-    take(0, 2)
-    pass_first(1)
-    multiply(0, 3, c)
-    pass_own(4)
-    take(0, 3)
-    pass_first(2)
-    complete(1)
-    multiply(0, 4, c)
-    multiply(1, 1, c)
-    take(0, 4)
-    pass_first(3)
-    complete(2)
-    multiply(1, 2, c)
-    take(1, 1)
-    complete(3)
-    multiply(1, 3, c)
-    take(1, 2)
-    outer_merge()
-    take(1, 3)
-    pass_first(4)
-    complete(4)
-    multiply(1, 4, c)
-    take(1, 4)
     keys[...] = acc[...].astype(BF16)
     for copy in sent:
         copy.wait_send()
@@ -390,7 +378,7 @@
     n_fsdp, n_rep = 4 * ny, 2 * nz
     slim, share = columns // n_rep, columns // nz
     nk = ny // 2
-    cut = rows // 2
+    cut = rows * 7 // 16
     hbm = pl.BlockSpec(memory_space=pltpu.HBM)
     vmem = pl.BlockSpec(memory_space=pltpu.VMEM)
     dma = pltpu.SemaphoreType.DMA
@@ -419,6 +407,7 @@
             pltpu.VMEM((nz - 1, share, rows), BF16),
             pltpu.VMEM((2, slim, rows), BF16),
             pltpu.VMEM((columns, rows), BF16),
+            pltpu.VMEM((slim, rows), F32),
             dma((7,)),
             dma((2, 3 * nk)), dma((2, 3 * nk)),
             dma((2 * nk + 2,)), dma((2 * nk + 2,)),

time: 52 us -> 46.8 us (0.90)
  Pallas kernels: 51.2 us -> 45.7 us
    pallas_call x1, Pallas kernels: 50.4 us -> 44.8 us  [shards(): pl.pallas_call(functools.partial(kernel, ny, nz, cut), out_shape=tuple((p...]
where the time goes in v3:
time: 46.8 us; the launch traced here: 46.3 us
  Pallas kernels  45.7 us (98%)
  between operations  0.64 us (1%)
    pallas_call x1, Pallas kernels, shards(): pl.pallas_call(functools.partial(kernel, ny, nz, cut), out_shape=tuple((p...  44.8 us

profile of v3, /device:TPU:1, one launch (start us, length us, event | category | flops | bytes accessed | tf_op | source)
XLA Modules:
  0.0 46.3 jit_solution(6427813414338806317)
XLA Ops:
  0.6 44.8 %shard_map.102 = (bf16[256,512]{1,0:T(8,128)(2,1)S(1)}, f32[32,256]{1,0:T(8,128)S(1)}, f32[32,256]{1,0:T(8,128)S(1)}, bf16[1,256,512]{2,1,0:T(8,128)(2,1)S(1)}) custom-call(bf16[256,8192]{1,0:T(8,128)(2,1)} %tok_hbm.1, f32[64,128]{1,0:T(8,128)} %bitcast.8, bf16[1,256,512]{2,1,0:T(8,128)(2,1)} %w_hbm.1, bf16[1,256,512]{2,1,0:T(8,128)(2,1)} %codes_hbm.1, ...), custom_call_target="tpu_custom_call" | custom-call | flops 2147483648 | bytes 4194304 | tf_op jit(solution)/shard_map/pallas_call | solution.py:391
  45.5 0.8 %shard_map.103 = (bf16[256,512]{1,0:T(8,128)(2,1)}, f32[32,256]{1,0:T(8,128)}, f32[32,256]{1,0:T(8,128)}, bf16[1,256,512]{2,1,0:T(8,128)(2,1)}) custom-call(bf16[256,512]{1,0:T(8,128)(2,1)S(1)} %get-tuple-element.12.keys, f32[32,256]{1,0:T(8,128)S(1)} %get-tuple-element.13.outer, f32[32,256]{1,0:T(8,128)S(1)} %get-tuple-element.14.mom, ...), custom_call_target="tpu_custom_call" | custom-call | tf_op jit(solution)/shard_map/pallas_call | solution.py:435

commit v4 on v3

--- a/solution.py
+++ b/solution.py
@@ -14,8 +14,8 @@
     "l0", "n0", "G1", "F1", "T1", "e0", "P0", "n1", "X0", "M0", "t0", "l1",
     "G2", "F2", "T2", "P1", "e1", "l2", "M1", "N0", "t1", "e2", "x0", "l3",
     "G3", "P2", "F3", "T3", "e3", "M2", "t2", "M3", "G4", "X1", "F4", "T4",
-    "t3", "P3", "M4", "N1", "t4", "X2", "N2", "x1", "X3", "N3", "x2", "P4",
-    "X4", "Z0", "N4", "x3", "x4",
+    "t3", "P3", "M4", "N1", "t4", "X2", "N2", "x1", "w0", "X3", "N3", "X4",
+    "x2", "P4", "x3", "N4", "x4", "Z0",
 )
 F32, BF16 = jnp.float32, jnp.bfloat16
 
@@ -54,9 +54,6 @@
         pltpu.make_async_copy(gain_hbm, gain, local_in.at[5]),
         pltpu.make_async_copy(tok_hbm, tok, local_in.at[6]),
     ]
-    for copy in inputs:
-        copy.start()
-
     barrier = pltpu.get_barrier_semaphore()
     near = [up, down, across, twin]
     far = [rep(z + j, xh) for j in range(1, nz)] + [rep(z, 1 - xh)]
@@ -68,6 +65,9 @@
         for other in near:
             pl.semaphore_signal(barrier, inc=1, device_id={"fsdp": other, "replica": me_r}, device_id_type=MESH)
 
+    for copy in inputs:
+        copy.start()
+
     @pl.when(jnp.logical_not(odd))
     def _():
         pl.semaphore_wait(barrier, len(near))
@@ -77,8 +77,6 @@
     @pl.when(odd)
     def _():
         pl.semaphore_wait(near_sem, len(near))
-        for other in far:
-            pl.semaphore_signal(barrier, inc=1, device_id={"fsdp": me_f, "replica": other}, device_id_type=MESH)
 
     def meet_far():
         @pl.when(odd)
@@ -98,7 +96,7 @@
         return full.at[owner, pl.ds(rr[0], rr[1]), pl.ds(cc[0], cc[1])]
 
     def copy_to(target, owner, rr, cc, send, recv, own=False):
-        source = w_hbm.at[0, pl.ds(rr[0], rr[1]), pl.ds(cc[0], cc[1])] if own else region(owner, rr, cc)
+        source = region(owner, rr, cc)
         return pltpu.make_async_remote_copy(
             src_ref=source,
             dst_ref=region(owner, rr, cc),
@@ -153,6 +151,10 @@
         index = twin_index(other, d, k)
         return copy_to(twin, fsdp(col, y - sign[d] * k, c), ALL, EVERY, d_send.at[index], d_recv.at[index],
                        own=(other == 0 and k == 0))
+
+    def last_copy(part, core):
+        index = 2 * ny - 1 + part
+        return copy_to(twin, fsdp(1 - xl, y - nk, core), (FIRST, SECOND)[part], EVERY, d_send.at[index], d_recv.at[index])
 
     def twin_arrived(other, d, k):
         col = 1 - xl if other else xl
@@ -175,6 +177,7 @@
 
         lax.fori_loop(0, count, one, 0)
 
+    inputs[0].wait()
     start(x_copy(0, 0))
     for d in (0, 1):
         start(y_copy(d, xl, 1, 1))
@@ -182,6 +185,11 @@
         start(y_copy(d, xl, 1, 0))
     start(x_copy(1, 0))
     start(twin_copy(0, 0, 0))
+
+    @pl.when(odd)
+    def _():
+        for other in far:
+            pl.semaphore_signal(barrier, inc=1, device_id={"fsdp": me_f, "replica": other}, device_id_type=MESH)
 
     share = columns // nz
     inputs[1].wait()
@@ -230,7 +238,6 @@
     inputs[4].wait()
     inputs[5].wait()
     inputs[6].wait()
-    inputs[0].wait()
     def ways(k):
         return (0, 1) if k < nk else (0,)
 
@@ -257,16 +264,25 @@
                 y_arrived(d, 1 - xl, k, 2)
                 if k < nk:
                     start(y_copy(d, 1 - xl, k + 1, 2))
+        if k == nk:
+            start(last_copy(0, c))
 
     def complete(k):
         for d in (0, 1) if k else (1,):
             x_arrived(d, k)
+        if k == nk:
+            start(last_copy(1, c))
+            return
         for d in ways(k) if k else (0,):
             start(twin_copy(1, d, k))
 
     def take(other, k):
-        for d in ways(k) if k else (0,):
-            twin_arrived(other, d, k)
+        if other and k == nk:
+            for part in (0, 1):
+                last_copy(part, 1 - c).wait_recv()
+        else:
+            for d in ways(k) if k else (0,):
+                twin_arrived(other, d, k)
         multiply(other, k, 1 - c)
 
     n_rep = nz * 2
@@ -338,6 +354,11 @@
             block = avg_blocks[b * LANES:(b + 1) * LANES, :].astype(F32).T
             own = full[me_f, :, b * LANES:(b + 1) * LANES].astype(F32)
             merged[0, :, b * LANES:(b + 1) * LANES] = (0.5 * own + 0.5 * block).astype(BF16)
+
+    def settle():
+        for copy in sent:
+            copy.wait_send()
+        sent.clear()
 
     early = jnp.logical_not(late)
     steps = {
@@ -354,13 +375,13 @@
         "e": lambda k: pl.when(early)((outer_send, outer_sum, outer_step, outer_spread)[k]),
         "l": lambda k: pl.when(late)((outer_send, outer_sum, outer_step, outer_spread)[k]),
         "Z": lambda k: outer_merge(),
+        "w": lambda k: settle(),
     }
     for step in ORDER:
         steps[step[0]](int(step[1]))
     sent.extend(spread_copies)
     keys[...] = acc[...].astype(BF16)
-    for copy in sent:
-        copy.wait_send()
+    settle()
 
 
 def write(keys, outer, mom, merged, keys_out, outer_out, mom_out, merged_out, sems):
@@ -411,7 +432,7 @@
             dma((7,)),
             dma((2, 3 * nk)), dma((2, 3 * nk)),
             dma((2 * nk + 2,)), dma((2 * nk + 2,)),
-            dma((2 * ny,)), dma((2 * ny,)),
+            dma((2 * ny + 1,)), dma((2 * ny + 1,)),
             dma((nz - 1,)), dma((nz - 1,)),
             dma((nz - 1,)), dma((nz - 1,)),
             dma((2,)), dma((2,)),

time: 46.8 us -> 46.7 us (level)
  no operation moved by 1% of the time
where the time goes in v4:
time: 46.7 us; the launch traced here: 46 us
  Pallas kernels  45.3 us (97%)
  between operations  0.64 us (1%)
    pallas_call x1, Pallas kernels, shards(): pl.pallas_call(functools.partial(kernel, ny, nz, cut), out_shape=tuple((p...  44.5 us

profile of v4, /device:TPU:1, one launch (start us, length us, event | category | flops | bytes accessed | tf_op | source)
XLA Modules:
  0.0 46.0 jit_solution(15017463018244153759)
XLA Ops:
  0.6 44.5 %shard_map.102 = (bf16[256,512]{1,0:T(8,128)(2,1)S(1)}, f32[32,256]{1,0:T(8,128)S(1)}, f32[32,256]{1,0:T(8,128)S(1)}, bf16[1,256,512]{2,1,0:T(8,128)(2,1)S(1)}) custom-call(bf16[256,8192]{1,0:T(8,128)(2,1)} %tok_hbm.1, f32[64,128]{1,0:T(8,128)} %bitcast.8, bf16[1,256,512]{2,1,0:T(8,128)(2,1)} %w_hbm.1, bf16[1,256,512]{2,1,0:T(8,128)(2,1)} %codes_hbm.1, ...), custom_call_target="tpu_custom_call" | custom-call | flops 2147483648 | bytes 4194304 | tf_op jit(solution)/shard_map/pallas_call | solution.py:412
  45.1 0.8 %shard_map.103 = (bf16[256,512]{1,0:T(8,128)(2,1)}, f32[32,256]{1,0:T(8,128)}, f32[32,256]{1,0:T(8,128)}, bf16[1,256,512]{2,1,0:T(8,128)(2,1)}) custom-call(bf16[256,512]{1,0:T(8,128)(2,1)S(1)} %get-tuple-element.12.keys, f32[32,256]{1,0:T(8,128)S(1)} %get-tuple-element.13.outer, f32[32,256]{1,0:T(8,128)S(1)} %get-tuple-element.14.mom, ...), custom_call_target="tpu_custom_call" | custom-call | tf_op jit(solution)/shard_map/pallas_call | solution.py:456

commit v5 on v4

--- a/solution.py
+++ b/solution.py
@@ -181,9 +181,9 @@
     start(x_copy(0, 0))
     for d in (0, 1):
         start(y_copy(d, xl, 1, 1))
+    start(x_copy(1, 0))
     for d in (0, 1):
         start(y_copy(d, xl, 1, 0))
-    start(x_copy(1, 0))
     start(twin_copy(0, 0, 0))
 
     @pl.when(odd)

time: 46.7 us -> 46.7 us (level)
  no operation moved by 1% of the time
where the time goes in v5:
time: 46.7 us; the launch traced here: 46 us
  Pallas kernels  45.3 us (97%)
  between operations  0.64 us (1%)
    pallas_call x1, Pallas kernels, shards(): pl.pallas_call(functools.partial(kernel, ny, nz, cut), out_shape=tuple((p...  44.5 us

profile of v5, /device:TPU:1, one launch (start us, length us, event | category | flops | bytes accessed | tf_op | source)
XLA Modules:
  0.0 46.0 jit_solution(734732305072136333)
XLA Ops:
  0.6 44.5 %shard_map.102 = (bf16[256,512]{1,0:T(8,128)(2,1)S(1)}, f32[32,256]{1,0:T(8,128)S(1)}, f32[32,256]{1,0:T(8,128)S(1)}, bf16[1,256,512]{2,1,0:T(8,128)(2,1)S(1)}) custom-call(bf16[256,8192]{1,0:T(8,128)(2,1)} %tok_hbm.1, f32[64,128]{1,0:T(8,128)} %bitcast.8, bf16[1,256,512]{2,1,0:T(8,128)(2,1)} %w_hbm.1, bf16[1,256,512]{2,1,0:T(8,128)(2,1)} %codes_hbm.1, ...), custom_call_target="tpu_custom_call" | custom-call | flops 2147483648 | bytes 4194304 | tf_op jit(solution)/shard_map/pallas_call | solution.py:412
  45.1 0.8 %shard_map.103 = (bf16[256,512]{1,0:T(8,128)(2,1)}, f32[32,256]{1,0:T(8,128)}, f32[32,256]{1,0:T(8,128)}, bf16[1,256,512]{2,1,0:T(8,128)(2,1)}) custom-call(bf16[256,512]{1,0:T(8,128)(2,1)S(1)} %get-tuple-element.12.keys, f32[32,256]{1,0:T(8,128)S(1)} %get-tuple-element.13.outer, f32[32,256]{1,0:T(8,128)S(1)} %get-tuple-element.14.mom, ...), custom_call_target="tpu_custom_call" | custom-call | tf_op jit(solution)/shard_map/pallas_call | solution.py:456
